TPU v7x, 512 devices: a whole 4x4x16 slice. The times are simulated.
512 devices in a mesh: row: 16 (over x, y), col: 32 (over z, core).
Axes of the slice: x: 4, y: 4, z: 16, core: 2. Of those that a mesh axis runs over, the one named last changes fastest.
Arguments:
- heights: float32 [2048, 8192], P('row', 'col'), may hold values from -6 to 6
- albedo: float32 [2048, 8192], P('row', 'col'), may hold values from 0.5 to 1.5
- images: float32 [8, 2048, 8192], P(None, 'row', 'col'), may hold values from 0.2 to 1.2
- lights: float32 [8, 2], replicated, may hold values from -0.7 to 0.7
Outputs:
- solution: float32 [2048, 8192], P('row', 'col')
- residual: float32 [2048, 8192], P('row', 'col')
All inputs are finite; a program needn't handle non-finite values.
Results may differ from a plain program's by a relative error of at most 0.0003.
Values sent between devices are 32-bit elements; how exact they have to be, the bound alone decides.
A program may use at most 64 MiB of HBM per device.

v0:
```python
import jax
import jax.numpy as jnp
from jax import lax
from jax.sharding import PartitionSpec as P

NIMG = 8
ITERS = 2


curvature_weight = 0.25
damping = 1.0


def with_halo(x, sides, width):
    for axis, dim in sides:
        count, length = (lax.axis_size(axis), x.shape[dim])
        up = [(i, (i + 1) % count) for i in range(count - 1)]
        down = [(j, i) for i, j in up]
        last = lax.slice_in_dim(x, length - width, length, axis=dim)
        initial = lax.slice_in_dim(x, 0, width, axis=dim)
        before = lax.ppermute(last, axis, up)
        after = lax.ppermute(initial, axis, down)
        x = jnp.concatenate([before, x, after], axis=dim)
    return x


def diff_cols(padded):
    return 0.5 * (padded[..., 1:-1, 2:] - padded[..., 1:-1, :-2])


def diff_rows(padded):
    return 0.5 * (padded[..., 2:, 1:-1] - padded[..., :-2, 1:-1])


def laplace(padded):
    centre = padded[..., 1:-1, 1:-1]
    return (
        padded[..., 2:, 1:-1]
        + padded[..., :-2, 1:-1]
        + padded[..., 1:-1, 2:]
        + padded[..., 1:-1, :-2]
        - 4.0 * centre
    )


def inner_halo(field):
    return with_halo(field, (("row", 0), ("col", 1)), 1)


def outer_halo(stacked):
    return with_halo(stacked, (("row", 1), ("col", 2)), 1)


def total_squares(residual):
    return lax.psum(jnp.sum(residual * residual), ("row", "col"))


def shards(heights, albedo, images, lights):
    padded_h = inner_halo(heights)
    slope_x = diff_cols(padded_h)
    slope_y = diff_rows(padded_h)
    laplace_h = laplace(padded_h)
    slant_sq = 1.0 + slope_x * slope_x + slope_y * slope_y
    slant_norm = jnp.sqrt(slant_sq)
    coef_xx = jnp.zeros_like(heights)
    coef_xy = jnp.zeros_like(heights)
    coef_yy = jnp.zeros_like(heights)
    flux_x = jnp.zeros_like(heights)
    flux_y = jnp.zeros_like(heights)
    for image_index in range(NIMG):
        light_x = lights[image_index, 0]
        light_y = lights[image_index, 1]
        norm_light = jnp.sqrt(1.0 + light_x * light_x + light_y * light_y)
        shading = albedo / (norm_light * slant_norm)
        facing = 1.0 - slope_x * light_x - slope_y * light_y
        mismatch = shading * facing - images[image_index]
        deriv_x = shading * (-light_x - facing * slope_x / slant_sq)
        deriv_y = shading * (-light_y - facing * slope_y / slant_sq)
        coef_xx = coef_xx + deriv_x * deriv_x
        coef_xy = coef_xy + deriv_x * deriv_y
        coef_yy = coef_yy + deriv_y * deriv_y
        flux_x = flux_x + deriv_x * mismatch
        flux_y = flux_y + deriv_y * mismatch
    outer_h = outer_halo(jnp.stack([flux_x, flux_y, laplace_h]))
    rhs = diff_cols(outer_h[0]) + diff_rows(outer_h[1]) - curvature_weight * laplace(outer_h[2])
    solution = jnp.zeros_like(rhs)
    residual = rhs
    direction = rhs
    norm_now = total_squares(residual)
    for iteration in range(ITERS):
        padded = inner_halo(direction)
        grad_x = diff_cols(padded)
        grad_y = diff_rows(padded)
        curvature = laplace(padded)
        weighted_x = coef_xx * grad_x + coef_xy * grad_y
        weighted_y = coef_xy * grad_x + coef_yy * grad_y
        outer = outer_halo(jnp.stack([weighted_x, weighted_y, curvature]))
        applied = (
            -(diff_cols(outer[0]) + diff_rows(outer[1]))
            + curvature_weight * laplace(outer[2])
            + damping * direction
        )
        step_size = norm_now / lax.psum(jnp.sum(direction * applied), ("row", "col"))
        solution = solution + step_size * direction
        residual = residual - step_size * applied
        norm_next = total_squares(residual)
        direction = residual + norm_next / norm_now * direction
        norm_now = norm_next
    return (solution, residual)


def solution(mesh):
    placed = (P("row", "col"), P("row", "col"), P(None, "row", "col"), P())
    return jax.shard_map(
        shards,
        mesh=mesh,
        in_specs=placed,
        out_specs=(P("row", "col"), P("row", "col")),
        check_vma=False,
    )
```

profile of v0, /device:TPU:1, one launch (start us, length us, event | category | flops | bytes accessed | tf_op | source)
XLA Modules:
  0.0 482.2 jit_solution(1268813580097036970)
XLA Ops:
  0.6 0.8 fusion.33
  1.5 4.0 collective-permute-start
  5.5 1.3 collective-permute-start.1
  6.8 2.0 fusion.34
  48.3 0.1 fusion.30
  48.4 4.4 collective-permute-start.3
  52.8 3.0 collective-permute-start.2
  55.9 2.5 collective-permute-done.2
  58.4 0.2 subtract_bitcast_fusion.2
  58.6 1.7 add_bitcast_fusion.5
  60.4 0.6 add_bitcast_fusion.4
  61.0 4.3 collective-permute-start.4
  65.2 1.3 collective-permute-start.5
  66.6 3.0 collective-permute-done.5
  69.6 0.1 fusion.27
  69.7 3.3 collective-permute-start.6
  73.0 1.9 collective-permute-start.7
  75.0 0.8 collective-permute-done.6
  75.8 4.4 collective-permute-done.7
  80.2 0.3 pad_maximum_fusion
  80.5 0.3 fusion.16
  80.9 3.2 collective-permute-start.8
  84.1 1.3 collective-permute-start.9
  85.4 3.8 collective-permute-done.9
  89.3 2.9 collective-permute-start.11
  92.2 1.9 collective-permute-start.10
  94.1 3.7 collective-permute-done.10
  97.8 0.2 subtract_bitcast_fusion.1
  98.0 0.2 add_bitcast_fusion.3
  98.2 0.2 add_bitcast_fusion.2
  98.4 5.7 %collective-permute-start.12 = (f32[3,1,256]{2,1,0:T(1,128)S(1)}, f32[3,1,256]{2,1,0:T(1,128)S(1)}, u32[]{:S(2)}, u32[]{:S(2)}) collective-permute-start(f32[3,1,256]{2,1,0:T(1,128)S(1)} %get-tuple-element.58), channel_id=1, source_target_pairs={{0,32},{32,64},{64,96},{96,128},{128,160},{160,192},{192,224},{224... | collective-permute-start | bytes 9224 | tf_op jit(solution)/shard_map/ppermute | solution.py:21
  104.2 1.3 collective-permute-start.13
  105.5 3.3 collective-permute-done.13
  108.8 0.1 fusion.26
  109.0 3.0 collective-permute-start.14
  112.0 1.9 collective-permute-start.15
  113.9 0.8 collective-permute-done.14
  114.7 4.4 collective-permute-done.15
  119.1 0.3 pad_maximum_fusion.1
  119.5 0.9 multiply_reduce_fusion.2
  120.4 114.7 %all-reduce = (f32[]{:T(128)}, f32[]{:T(128)}) all-reduce(f32[]{:T(128)} %get-tuple-element.3, f32[]{:T(128)} %get-tuple-element.2), channel_id=1, replica_groups=mesh['row'=16,'col'=32] {'row','col'}, use_global_device_ids=true, to_apply=%region_1.0 | all-reduce | flops 2 | bytes 16 | tf_op jit(solution)/shard_map/psum | solution.py:55
  236.5 0.6 multiply_reduce_fusion.1
  237.1 98.6 %psum.30 = f32[]{:T(128)} all-reduce(f32[]{:T(128)} %multiply_reduce_fusion.1), channel_id=1, replica_groups=mesh['row'=16,'col'=32] {'row','col'}, use_global_device_ids=true, to_apply=%region_5.0 | all-reduce | flops 1 | bytes 8 | tf_op jit(solution)/shard_map/psum | solution.py:55
  337.1 3.0 collective-permute-start.16
  340.1 1.3 collective-permute-start.17
  341.4 3.0 collective-permute-done.17
  344.5 5.6 %collective-permute-start.19 = (f32[130,1]{1,0:T(8,128)S(1)}, f32[130,1]{1,0:T(8,128)S(1)}, u32[]{:S(2)}, u32[]{:S(2)}) collective-permute-start(f32[130,1]{1,0:T(8,128)S(1)} %get-tuple-element.62), channel_id=1, source_target_pairs={{0,1},{1,2},{2,3},{3,4},{4,5},{5,6},{6,7},{7,8},{8,9},{9,10},{10,1... | collective-permute-start | bytes 1568 | tf_op jit(solution)/shard_map/ppermute | solution.py:21
  350.1 1.9 collective-permute-start.18
  352.1 3.7 collective-permute-done.18
  355.8 0.2 subtract_bitcast_fusion
  355.9 0.2 add_bitcast_fusion.1
  356.1 0.2 add_bitcast_fusion
  356.3 2.3 collective-permute-start.20
  358.6 1.3 collective-permute-start.21
  359.9 3.3 collective-permute-done.21
  363.2 0.1 fusion.25
  363.3 3.0 collective-permute-start.22
  366.4 1.9 collective-permute-start.23
  368.3 0.8 collective-permute-done.22
  369.1 4.4 collective-permute-done.23
  373.5 0.3 pad_maximum_fusion.2
  373.8 0.9 multiply_reduce_fusion
  374.8 105.3 %psum.31 = f32[]{:T(128)} all-reduce(f32[]{:T(128)} %get-tuple-element.6), channel_id=1, replica_groups=mesh['row'=16,'col'=32] {'row','col'}, use_global_device_ids=true, to_apply=%region_7.0 | all-reduce | flops 1 | bytes 8 | tf_op jit(solution)/shard_map/psum | solution.py:103
  481.4 0.7 multiply_subtract_fusion
  (33 shorter events, 0.6 us)
Async XLA Ops:
  0.6 47.7 %copy-start = (f32[128,256]{1,0:T(8,128)S(1)}, f32[128,256]{1,0:T(8,128)}, u32[]{:S(2)}) copy-start(f32[128,256]{1,0:T(8,128)} %param.4) | copy-start | bytes 393220
  0.6 57.9 %copy-start.1 = (f32[8,128,256]{2,1,0:T(8,128)S(1)}, f32[8,128,256]{2,1,0:T(8,128)}, u32[]{:S(2)}) copy-start(f32[8,128,256]{2,1,0:T(8,128)} %param.6) | copy-start | bytes 3145732
  1.5 46.8 %collective-permute-start = (f32[1,256]{1,0:T(1,128)S(1)}, f32[1,256]{1,0:T(1,128)S(1)}, u32[]{:S(2)}, u32[]{:S(2)}) collective-permute-start(f32[1,256]{1,0:T(1,128)S(1)} %get-tuple-element.74), channel_id=1, source_target_pairs={{0,32},{32,64},{64,96},{96,128},{128,160},{160,192},{192,224},{224... | collective-permute-start | bytes 3080 | tf_op jit(solution)/shard_map/ppermute | solution.py:21
  5.5 42.8 %collective-permute-start.1 = (f32[1,256]{1,0:T(1,128)S(1)}, f32[1,256]{1,0:T(1,128)S(1)}, u32[]{:S(2)}, u32[]{:S(2)}) collective-permute-start(f32[1,256]{1,0:T(1,128)S(1)} %get-tuple-element.75), channel_id=1, source_target_pairs={{32,0},{64,32},{96,64},{128,96},{160,128},{192,160},{224,192},{256... | collective-permute-start | bytes 3080 | tf_op jit(solution)/shard_map/ppermute | solution.py:22
  48.4 7.5 %collective-permute-start.3 = (f32[130,1]{1,0:T(8,128)S(1)}, f32[130,1]{1,0:T(8,128)S(1)}, u32[]{:S(2)}, u32[]{:S(2)}) collective-permute-start(f32[130,1]{1,0:T(8,128)S(1)} %get-tuple-element.66), channel_id=1, source_target_pairs={{0,1},{1,2},{2,3},{3,4},{4,5},{5,6},{6,7},{7,8},{8,9},{9,10},{10,1... | collective-permute-start | bytes 1568 | tf_op jit(solution)/shard_map/ppermute | solution.py:21
  52.8 5.6 %collective-permute-start.2 = (f32[130,1]{1,0:T(8,128)S(1)}, f32[130,1]{1,0:T(8,128)S(1)}, u32[]{:S(2)}, u32[]{:S(2)}) collective-permute-start(f32[130,1]{1,0:T(8,128)S(1)} %get-tuple-element.67), channel_id=1, source_target_pairs={{1,0},{2,1},{3,2},{4,3},{5,4},{6,5},{7,6},{8,7},{9,8},{10,9},{11,1... | collective-permute-start | bytes 1568 | tf_op jit(solution)/shard_map/ppermute | solution.py:22
  58.6 1.8 copy-start.2
  61.0 5.6 %collective-permute-start.4 = (f32[3,1,256]{2,1,0:T(1,128)S(1)}, f32[3,1,256]{2,1,0:T(1,128)S(1)}, u32[]{:S(2)}, u32[]{:S(2)}) collective-permute-start(f32[3,1,256]{2,1,0:T(1,128)S(1)} %get-tuple-element.60), channel_id=1, source_target_pairs={{0,32},{32,64},{64,96},{96,128},{128,160},{160,192},{192,224},{224... | collective-permute-start | bytes 9224 | tf_op jit(solution)/shard_map/ppermute | solution.py:21
  65.2 4.3 collective-permute-start.5
  69.7 6.0 %collective-permute-start.6 = (f32[3,130,1]{2,1,0:T(8,128)S(1)}, f32[3,130,1]{2,1,0:T(8,128)S(1)}, u32[]{:S(2)}, u32[]{:S(2)}) collective-permute-start(f32[3,130,1]{2,1,0:T(8,128)S(1)} %get-tuple-element.54), channel_id=1, source_target_pairs={{0,1},{1,2},{2,3},{3,4},{4,5},{5,6},{6,7},{7,8},{8,9},{9,10},{10,1... | collective-permute-start | bytes 4688 | tf_op jit(solution)/shard_map/ppermute | solution.py:21
  73.0 7.1 %collective-permute-start.7 = (f32[3,130,1]{2,1,0:T(8,128)S(1)}, f32[3,130,1]{2,1,0:T(8,128)S(1)}, u32[]{:S(2)}, u32[]{:S(2)}) collective-permute-start(f32[3,130,1]{2,1,0:T(8,128)S(1)} %get-tuple-element.55), channel_id=1, source_target_pairs={{1,0},{2,1},{3,2},{4,3},{5,4},{6,5},{7,6},{8,7},{9,8},{10,9},{11,1... | collective-permute-start | bytes 4688 | tf_op jit(solution)/shard_map/ppermute | solution.py:22
  80.9 4.5 collective-permute-start.8
  84.1 5.1 %collective-permute-start.9 = (f32[1,256]{1,0:T(1,128)S(1)}, f32[1,256]{1,0:T(1,128)S(1)}, u32[]{:S(2)}, u32[]{:S(2)}) collective-permute-start(f32[1,256]{1,0:T(1,128)S(1)} %get-tuple-element.73), channel_id=1, source_target_pairs={{32,0},{64,32},{96,64},{128,96},{160,128},{192,160},{224,192},{256... | collective-permute-start | bytes 3080 | tf_op jit(solution)/shard_map/ppermute | solution.py:22
  89.3 4.8 %collective-permute-start.11 = (f32[130,1]{1,0:T(8,128)S(1)}, f32[130,1]{1,0:T(8,128)S(1)}, u32[]{:S(2)}, u32[]{:S(2)}) collective-permute-start(f32[130,1]{1,0:T(8,128)S(1)} %get-tuple-element.64), channel_id=1, source_target_pairs={{0,1},{1,2},{2,3},{3,4},{4,5},{5,6},{6,7},{7,8},{8,9},{9,10},{10,1... | collective-permute-start | bytes 1568 | tf_op jit(solution)/shard_map/ppermute | solution.py:21
  92.2 5.6 %collective-permute-start.10 = (f32[130,1]{1,0:T(8,128)S(1)}, f32[130,1]{1,0:T(8,128)S(1)}, u32[]{:S(2)}, u32[]{:S(2)}) collective-permute-start(f32[130,1]{1,0:T(8,128)S(1)} %get-tuple-element.65), channel_id=1, source_target_pairs={{1,0},{2,1},{3,2},{4,3},{5,4},{6,5},{7,6},{8,7},{9,8},{10,9},{11,1... | collective-permute-start | bytes 1568 | tf_op jit(solution)/shard_map/ppermute | solution.py:22
  98.4 7.1 %collective-permute-start.12 = (f32[3,1,256]{2,1,0:T(1,128)S(1)}, f32[3,1,256]{2,1,0:T(1,128)S(1)}, u32[]{:S(2)}, u32[]{:S(2)}) collective-permute-start(f32[3,1,256]{2,1,0:T(1,128)S(1)} %get-tuple-element.58), channel_id=1, source_target_pairs={{0,32},{32,64},{64,96},{96,128},{128,160},{160,192},{192,224},{224... | collective-permute-start | bytes 9224 | tf_op jit(solution)/shard_map/ppermute | solution.py:21
  104.2 4.6 collective-permute-start.13
  109.0 5.7 %collective-permute-start.14 = (f32[3,130,1]{2,1,0:T(8,128)S(1)}, f32[3,130,1]{2,1,0:T(8,128)S(1)}, u32[]{:S(2)}, u32[]{:S(2)}) collective-permute-start(f32[3,130,1]{2,1,0:T(8,128)S(1)} %get-tuple-element.52), channel_id=1, source_target_pairs={{0,1},{1,2},{2,3},{3,4},{4,5},{5,6},{6,7},{7,8},{8,9},{9,10},{10,1... | collective-permute-start | bytes 4688 | tf_op jit(solution)/shard_map/ppermute | solution.py:21
  112.0 7.1 %collective-permute-start.15 = (f32[3,130,1]{2,1,0:T(8,128)S(1)}, f32[3,130,1]{2,1,0:T(8,128)S(1)}, u32[]{:S(2)}, u32[]{:S(2)}) collective-permute-start(f32[3,130,1]{2,1,0:T(8,128)S(1)} %get-tuple-element.53), channel_id=1, source_target_pairs={{1,0},{2,1},{3,2},{4,3},{5,4},{6,5},{7,6},{8,7},{9,8},{10,9},{11,1... | collective-permute-start | bytes 4688 | tf_op jit(solution)/shard_map/ppermute | solution.py:22
  337.1 4.3 collective-permute-start.16
  340.1 4.3 collective-permute-start.17
  344.5 7.5 %collective-permute-start.19 = (f32[130,1]{1,0:T(8,128)S(1)}, f32[130,1]{1,0:T(8,128)S(1)}, u32[]{:S(2)}, u32[]{:S(2)}) collective-permute-start(f32[130,1]{1,0:T(8,128)S(1)} %get-tuple-element.62), channel_id=1, source_target_pairs={{0,1},{1,2},{2,3},{3,4},{4,5},{5,6},{6,7},{7,8},{8,9},{9,10},{10,1... | collective-permute-start | bytes 1568 | tf_op jit(solution)/shard_map/ppermute | solution.py:21
  350.1 5.6 %collective-permute-start.18 = (f32[130,1]{1,0:T(8,128)S(1)}, f32[130,1]{1,0:T(8,128)S(1)}, u32[]{:S(2)}, u32[]{:S(2)}) collective-permute-start(f32[130,1]{1,0:T(8,128)S(1)} %get-tuple-element.63), channel_id=1, source_target_pairs={{1,0},{2,1},{3,2},{4,3},{5,4},{6,5},{7,6},{8,7},{9,8},{10,9},{11,1... | collective-permute-start | bytes 1568 | tf_op jit(solution)/shard_map/ppermute | solution.py:22
  356.3 3.6 collective-permute-start.20
  358.6 4.6 collective-permute-start.21
  363.3 5.7 %collective-permute-start.22 = (f32[3,130,1]{2,1,0:T(8,128)S(1)}, f32[3,130,1]{2,1,0:T(8,128)S(1)}, u32[]{:S(2)}, u32[]{:S(2)}) collective-permute-start(f32[3,130,1]{2,1,0:T(8,128)S(1)} %get-tuple-element.50), channel_id=1, source_target_pairs={{0,1},{1,2},{2,3},{3,4},{4,5},{5,6},{6,7},{7,8},{8,9},{9,10},{10,1... | collective-permute-start | bytes 4688 | tf_op jit(solution)/shard_map/ppermute | solution.py:21
  366.4 7.1 %collective-permute-start.23 = (f32[3,130,1]{2,1,0:T(8,128)S(1)}, f32[3,130,1]{2,1,0:T(8,128)S(1)}, u32[]{:S(2)}, u32[]{:S(2)}) collective-permute-start(f32[3,130,1]{2,1,0:T(8,128)S(1)} %get-tuple-element.51), channel_id=1, source_target_pairs={{1,0},{2,1},{3,2},{4,3},{5,4},{6,5},{7,6},{8,7},{9,8},{10,9},{11,1... | collective-permute-start | bytes 4688 | tf_op jit(solution)/shard_map/ppermute | solution.py:22
where the time goes:
time: 484 us; the launch traced here: 482 us
  blocking collectives  319 us (66%)
  starting transfers between devices  65 us (13%)
  between operations  44.8 us (9%)
  waiting for transfers between devices  41.9 us (9%)
  other arithmetic  8.19 us (2%)
    psum x2, blocking collectives, total_squares(): return lax.psum(jnp.sum(residual * residual), ('row', 'col'))  213 us
    psum x1, blocking collectives, shards(): lax.psum(jnp.sum(direction * applied), ('row', 'col'))  105 us
    ppermute x12, starting transfers between devices, with_halo(): before = lax.ppermute(last, axis, up)  44.7 us
    ppermute x12, waiting for transfers between devices, with_halo(): after = lax.ppermute(initial, axis, down)  39.5 us
    ppermute x12, starting transfers between devices, with_halo(): after = lax.ppermute(initial, axis, down)  20.3 us
  transfers between devices with their start and end apart: 24, of which 14 were waited for; matrix products, arithmetic and copies ran while one was open for 0% of the time, Pallas kernels for 0%

commit v1 on v0

v1 whole, which is shorter than its diff:
```python
import jax
import jax.numpy as jnp
from jax import lax
from jax.experimental import pallas as pl
from jax.experimental.pallas import tpu as pltpu
from jax.sharding import PartitionSpec as P

MESH = pl.DeviceIdType.MESH
F32 = jnp.float32
NIMG = 8
NR, NC = 16, 32
ROWS, COLS = 128, 256
TILES = ROWS // 8
NF = 5
TOP = 16
STRIDE = 12


def kernel(
    heights, albedo, images, lights, sol_out, res_out,
    fields, img, light, packs, strips, corners, coef, xs, yp, ym, vec_r, vec_u, vec_w, part, sums_row, sums_col,
    in_sem, img_sem, send_sem, recv_sem, ar_send, ar_recv,
):
    row, col = lax.axis_index("row"), lax.axis_index("col")

    def dev(dr, dc):
        return (lax.rem(row + (dr + NR), NR), lax.rem(col + (dc + NC), NC))

    loads = []
    for f, src in enumerate((heights, albedo)):
        for t in range(2):
            loads.append(
                pltpu.make_async_copy(src.at[:, pl.ds(128 * t, 128)], fields.at[f, t, pl.ds(TOP, ROWS), :], in_sem.at[2 * f + t])
            )
    load_light = pltpu.make_async_copy(lights, light, in_sem.at[4])
    load_img = [pltpu.make_async_copy(images.at[k], img.at[k], img_sem.at[k]) for k in range(NIMG)]
    load_light.start()
    for cp in load_img:
        cp.start()
    for cp in loads:
        cp.start()

    peers = {(a, b) for a in (-1, 0, 1) for b in (-1, 0, 1)} | {(d, 0) for d in range(NR)} | {(0, d) for d in range(NC)}
    peers = sorted({(a % NR, b % NC) for a, b in peers} - {(0, 0)})
    barrier = pltpu.get_barrier_semaphore()
    for p in peers:
        pl.semaphore_signal(barrier, inc=1, device_id=dev(*p), device_id_type=MESH)

    lane = lax.broadcasted_iota(jnp.int32, (8, 128), 1)
    zero = jnp.zeros((8, 128), F32)
    for t in range(3):
        for ref in (fields.at[0], yp, ym, vec_r, vec_u):
            ref[t, pl.ds(0, 8), :] = zero
            ref[t, pl.ds(ROWS + 24, 8), :] = zero

    load_light.wait()
    lx, ly = light[0:1, :], light[1:2, :]
    inv_sq = 1.0 / (1.0 + lx * lx + ly * ly)
    inv_norm = jnp.sqrt(inv_sq)

    def over_images(x):
        return jnp.broadcast_to(jnp.sum(x, axis=1, keepdims=True), (8, 128))

    m00, m10, m01 = over_images(inv_sq), over_images(inv_sq * lx), over_images(inv_sq * ly)
    m20, m11, m02 = over_images(inv_sq * lx * lx), over_images(inv_sq * lx * ly), over_images(inv_sq * ly * ly)
    weights = [
        [jnp.broadcast_to(w[:, k : k + 1], (8, 128)) for w in (inv_norm, inv_norm * lx, inv_norm * ly)] for k in range(NIMG)
    ]

    for cp in load_img:
        cp.wait()

    def image_sums(i, carry):
        at = pl.ds(pl.multiple_of(8 * i, 8), 8)
        to = pl.ds(pl.multiple_of(8 * i + TOP, 8), 8)
        for t in range(2):
            acc = [zero, zero, zero]
            for k in range(NIMG):
                v = img[k, at, pl.ds(128 * t, 128)]
                acc = [acc[j] + weights[k][j] * v for j in range(3)]
            for j in range(3):
                fields[2 + j, t, to, :] = acc[j]
        return carry

    lax.fori_loop(0, TILES, image_sums, 0, unroll=2)
    for cp in loads:
        cp.wait()

    shifts = [(64 * g + STRIDE * f, g, f) for g in range(2) for f in range(NF)]

    def pack(j, carry):
        left, right, first = zero, zero, None
        for s, g, f in shifts:
            at = pl.ds(pl.multiple_of(8 * j + (64 * g + TOP), 8), 8)
            a, b = fields[f, 0, at, :], fields[f, 1, at, :]
            if s:
                a, b = pltpu.roll(a, s, 1), pltpu.roll(b, s, 1)
                left = jnp.where(lane >= s, a, left)
                right = jnp.where(lane >= s - 6, b, right)
            else:
                left, right, first = a, b, b
        to = pl.ds(pl.multiple_of(8 * j, 8), 8)
        packs[0, to, :] = left
        packs[1, to, :] = jnp.where(lane >= 122, first, right)
        return carry

    lax.fori_loop(0, 8, pack, 0, unroll=2)

    pl.semaphore_wait(barrier, len(peers))
    first8, last8 = pl.ds(0, 8), pl.ds(56, 8)
    moves = [
        (packs.at[0, first8, :], corners.at[1, 0], (-1, -1)),
        (packs.at[1, first8, :], corners.at[1, 1], (-1, 1)),
        (packs.at[0, last8, :], corners.at[0, 0], (1, -1)),
        (packs.at[1, last8, :], corners.at[0, 1], (1, 1)),
        (fields.at[:, pl.ds(0, 2), pl.ds(TOP, 8), :], fields.at[:, pl.ds(0, 2), pl.ds(TOP + ROWS, 8), :], (-1, 0)),
        (fields.at[:, pl.ds(0, 2), pl.ds(TOP + ROWS - 8, 8), :], fields.at[:, pl.ds(0, 2), pl.ds(TOP - 8, 8), :], (1, 0)),
        (packs.at[0], strips.at[0], (0, -1)),
        (packs.at[1], strips.at[1], (0, 1)),
    ]
    copies = [
        pltpu.make_async_remote_copy(
            src_ref=src, dst_ref=dst, send_sem=send_sem.at[n], recv_sem=recv_sem.at[n], device_id=dev(*to), device_id_type=MESH
        )
        for n, (src, dst, to) in enumerate(moves)
    ]
    for cp in copies:
        cp.start()
    for cp in copies:
        cp.wait()

    above = jnp.where(row > 0, 1.0, 0.0).astype(F32)
    below = jnp.where(row < NR - 1, 1.0, 0.0).astype(F32)
    before = jnp.where(col > 0, 1.0, 0.0).astype(F32)
    after = jnp.where(col < NC - 1, 1.0, 0.0).astype(F32)
    side_mask = jnp.where(lane < 64, after, before)

    def masks(e):
        m = jnp.where(e == 0, above, jnp.where(e == TILES + 1, below, 1.0))
        return (m, m, m * side_mask)

    in_group = lane & 63
    from_right = in_group < 6
    for f in range(1, NF):
        from_right = from_right | ((in_group >= STRIDE * f) & (in_group < STRIDE * f + 6))

    def side(merged, g, f, at, mask):
        s = 64 * g + STRIDE * f
        v = pltpu.roll(merged, 128 - s, 1) if s else merged
        fields[f, 2, at, :] = v * mask if f < 2 else v

    def unpack(j, carry):
        at = pl.ds(pl.multiple_of(8 * j, 8), 8)
        merged = jnp.where(from_right, strips[0, at, :], strips[1, at, :])
        for s, g, f in shifts:
            side(merged, g, f, pl.ds(pl.multiple_of(8 * j + (64 * g + TOP), 8), 8), side_mask)
        return carry

    lax.fori_loop(0, 8, unpack, 0, unroll=2)
    for b, g, start, ok in ((0, 1, TOP - 8, above), (1, 0, TOP + ROWS, below)):
        merged = jnp.where(from_right, corners[b, 0], corners[b, 1])
        at = pl.ds(start, 8)
        for f in range(NF):
            side(merged, g, f, at, side_mask * ok)
        for f in range(2):
            for t in range(2):
                fields[f, t, at, :] = fields[f, t, at, :] * ok

    is_last, is_first = lane == 127, lane == 0

    def nexts(v):
        r = [pltpu.roll(x, 127, 1) for x in v]
        return [jnp.where(is_last, r[(t + 1) % 3], r[t]) for t in range(3)]

    def prevs(v):
        r = [pltpu.roll(x, 1, 1) for x in v]
        return [jnp.where(is_first, r[(t + 2) % 3], r[t]) for t in range(3)]

    def scatter(e, q, hx, hy):
        n = nexts([q[t] - hx[t] for t in range(3)])
        p = prevs([q[t] + hx[t] for t in range(3)])
        at, to = pl.ds(pl.multiple_of(8 * e, 8), 8), pl.ds(pl.multiple_of(8 * e + 8, 8), 8)
        for t in range(3):
            xs[t, at, :] = n[t] + p[t] - 4.0 * q[t]
            yp[t, to, :] = q[t] - hy[t]
            ym[t, to, :] = q[t] + hy[t]

    def stencil(ref, e):
        base = 8 * e + 8
        v = [ref[t, pl.ds(pl.multiple_of(base, 8), 8), :] for t in range(3)]
        up = [ref[t, pl.ds(base - 1, 8), :] for t in range(3)]
        down = [ref[t, pl.ds(base + 1, 8), :] for t in range(3)]
        n, p = nexts(v), prevs(v)
        m = masks(e)
        q = [(0.25 * m[t]) * ((n[t] + p[t]) + (up[t] + down[t]) - 4.0 * v[t]) for t in range(3)]
        gx = [n[t] - p[t] for t in range(3)]
        gy = [down[t] - up[t] for t in range(3)]
        return q, gx, gy

    def gather(e, t):
        base = 8 * e + 8
        return xs[t, pl.ds(pl.multiple_of(8 * e, 8), 8), :] + yp[t, pl.ds(base + 1, 8), :] + ym[t, pl.ds(base - 1, 8), :]

    def linearize(e, carry):
        q, gx, gy = stencil(fields.at[0], e)
        at, to = pl.ds(pl.multiple_of(8 * e + 8, 8), 8), pl.ds(pl.multiple_of(8 * e, 8), 8)
        hx, hy = [], []
        for t in range(3):
            sx, sy = 0.5 * gx[t], 0.5 * gy[t]
            inv = 1.0 / (1.0 + sx * sx + sy * sy)
            a = fields[1, t, at, :] * jnp.sqrt(inv)
            j0, jx, jy = fields[2, t, at, :], fields[3, t, at, :], fields[4, t, at, :]
            tx, ty = sx * inv, sy * inv
            f1x = m10 - sx * m20 - sy * m11
            f1y = m01 - sx * m11 - sy * m02
            f2 = m00 - sx * m10 - sy * m01 - sx * f1x - sy * f1y
            g1x, g1y = f1x + tx * f2, f1y + ty * f2
            jf = j0 - sx * jx - sy * jy
            qa = 0.25 * (a * a)
            coef[0, t, to, :] = qa * (m20 + tx * (f1x + g1x))
            coef[1, t, to, :] = qa * (m11 + ty * f1x + tx * g1y)
            coef[2, t, to, :] = qa * (m02 + ty * (f1y + g1y))
            ha = 0.5 * a
            hx.append(ha * (jx + tx * jf - a * g1x))
            hy.append(ha * (jy + ty * jf - a * g1y))
        scatter(e, q, hx, hy)
        return carry

    def right_side(e, carry):
        m, at = masks(e), pl.ds(pl.multiple_of(8 * e + 8, 8), 8)
        for t in range(3):
            vec_r[t, at, :] = -m[t] * gather(e, t)
        return carry

    def apply_from(ref):
        def body(e, carry):
            q, gx, gy = stencil(ref, e)
            at = pl.ds(pl.multiple_of(8 * e, 8), 8)
            cxx, cxy, cyy = ([coef[j, t, at, :] for t in range(3)] for j in range(3))
            hx = [cxx[t] * gx[t] + cxy[t] * gy[t] for t in range(3)]
            hy = [cxy[t] * gx[t] + cyy[t] * gy[t] for t in range(3)]
            scatter(e, q, hx, hy)
            return carry

        return body

    def image_of_r(e, carry):
        m, at = masks(e), pl.ds(pl.multiple_of(8 * e + 8, 8), 8)
        for t in range(3):
            vec_u[t, at, :] = m[t] * gather(e, t)
        return carry

    def image_of_u(e, acc):
        at = pl.ds(pl.multiple_of(8 * e + 8, 8), 8)
        for t in range(2):
            w = gather(e, t)
            r, u = vec_r[t, at, :], vec_u[t, at, :]
            vec_w[t, pl.ds(pl.multiple_of(8 * e - 8, 8), 8), :] = w
            acc = (acc[0] + r * r, acc[1] + r * u, acc[2] + u * u, acc[3] + u * w)
        return acc

    lax.fori_loop(0, TILES + 2, linearize, 0, unroll=2)
    lax.fori_loop(0, TILES + 2, right_side, 0, unroll=3)
    lax.fori_loop(0, TILES + 2, apply_from(vec_r), 0, unroll=2)
    lax.fori_loop(0, TILES + 2, image_of_r, 0, unroll=3)
    lax.fori_loop(0, TILES + 2, apply_from(vec_u), 0, unroll=2)
    acc = lax.fori_loop(1, TILES + 1, image_of_u, (zero, zero, zero, zero), unroll=4)

    folded = []
    for x in acc:
        x = x + pltpu.roll(x, 64, 1)
        folded.append(x + pltpu.roll(x, 32, 1))
    mixed = jnp.where(lane < 64, jnp.where(lane < 32, folded[0], folded[1]), jnp.where(lane < 96, folded[2], folded[3]))
    mine = jnp.sum(mixed, axis=0, keepdims=True)

    def exchange(stage, mine, slots, count, target):
        part[stage] = mine
        out = [
            pltpu.make_async_remote_copy(
                src_ref=part.at[stage], dst_ref=slots.at[d - 1], send_sem=ar_send.at[stage], recv_sem=ar_recv.at[stage],
                device_id=target(d), device_id_type=MESH,
            )
            for d in range(1, count)
        ]
        for cp in out:
            cp.start()
        pltpu.make_async_copy(slots, slots, ar_recv.at[stage]).wait()
        total = mine
        for d in range(1, count):
            total = total + slots[d - 1]
        return total

    total = exchange(0, mine, sums_row, NR, lambda d: dev(d, 0))
    total = exchange(1, total, sums_col, NC, lambda d: dev(0, d))
    pltpu.make_async_copy(sums_row, sums_row, ar_send.at[0]).wait()
    pltpu.make_async_copy(sums_col, sums_col, ar_send.at[1]).wait()

    lane1 = lax.broadcasted_iota(jnp.int32, (1, 128), 1)

    def quarter(n):
        picked = jnp.where((lane1 >= 32 * n) & (lane1 < 32 * n + 32), total, 0.0)
        return jnp.broadcast_to(jnp.sum(picked, axis=1, keepdims=True), (8, 128))

    rr, ru, uu, uw = (quarter(n) for n in range(4))
    p1, p2, p3 = ru / rr, uu / rr, uw / rr
    step0 = 1.0 / (1.0 + p1)
    keep = p1 * step0
    beta = (p2 - p1 * p1) * (step0 * step0)
    g = keep + beta
    curve = g * g * (1.0 + p1) - 2.0 * g * step0 * (p1 + p2) + step0 * step0 * (p2 + p3)
    step1 = beta / curve
    s_r, s_u = step0 + step1 * g, -step1 * step0
    d_r, d_u, d_w = keep - step1 * g, -step0 - step1 * (g - step0), step1 * step0

    def finish(i, carry):
        at, to = pl.ds(pl.multiple_of(8 * i, 8), 8), pl.ds(pl.multiple_of(8 * i + TOP, 8), 8)
        for t in range(2):
            r, u, w = vec_r[t, to, :], vec_u[t, to, :], vec_w[t, at, :]
            sol_out[at, pl.ds(128 * t, 128)] = s_r * r + s_u * u
            res_out[at, pl.ds(128 * t, 128)] = d_r * r + d_u * u + d_w * w
        return carry

    lax.fori_loop(0, TILES, finish, 0, unroll=4)


def shards(heights, albedo, images, lights):
    padded = pltpu.VMEM((3, ROWS + 32, 128), F32)
    return pl.pallas_call(
        kernel,
        out_shape=[jax.ShapeDtypeStruct((ROWS, COLS), F32)] * 2,
        in_specs=[pl.BlockSpec(memory_space=pltpu.HBM)] * 4,
        out_specs=[pl.BlockSpec(memory_space=pltpu.VMEM)] * 2,
        scratch_shapes=[
            pltpu.VMEM((NF, 3, ROWS + 32, 128), F32),
            pltpu.VMEM((NIMG, ROWS, COLS), F32),
            pltpu.VMEM((2, NIMG), F32),
            pltpu.VMEM((2, ROWS // 2, 128), F32),
            pltpu.VMEM((2, ROWS // 2, 128), F32),
            pltpu.VMEM((2, 2, 8, 128), F32),
            pltpu.VMEM((3, 3, ROWS + 16, 128), F32),
            pltpu.VMEM((3, ROWS + 16, 128), F32),
            padded, padded, padded, padded,
            pltpu.VMEM((2, ROWS, 128), F32),
            pltpu.VMEM((2, 1, 128), F32),
            pltpu.VMEM((NR - 1, 1, 128), F32),
            pltpu.VMEM((NC - 1, 1, 128), F32),
            pltpu.SemaphoreType.DMA((5,)),
            pltpu.SemaphoreType.DMA((NIMG,)),
            pltpu.SemaphoreType.DMA((8,)),
            pltpu.SemaphoreType.DMA((8,)),
            pltpu.SemaphoreType.DMA((2,)),
            pltpu.SemaphoreType.DMA((2,)),
        ],
        compiler_params=pltpu.CompilerParams(collective_id=0, has_side_effects=True, vmem_limit_bytes=40 * 1024 * 1024),
    )(heights, albedo, images, lights.T)


def solution(mesh):
    placed = (P("row", "col"), P("row", "col"), P(None, "row", "col"), P())
    return jax.shard_map(
        shards, mesh=mesh, in_specs=placed, out_specs=(P("row", "col"), P("row", "col")), check_vma=False
    )
```

time: 484 us -> 45.8 us (0.09)
  blocking collectives: 319 us -> 0 us
  starting transfers between devices: 65 us -> 0 us
  between operations: 44.8 us -> 0.65 us
  waiting for transfers between devices: 41.9 us -> 0 us
  Pallas kernels: 0 us -> 39.9 us
  other arithmetic: 8.19 us -> 0 us
    psum x3 -> x0, blocking collectives: 319 us -> none  [the longest x2 213 us: total_squares(): return lax.psum(jnp.sum(residual * residual), ('row', 'col'))]
    ppermute x24 -> x0, starting transfers between devices: 65 us -> none  [the longest x12 44.7 us: with_halo(): before = lax.ppermute(last, axis, up)]
    ppermute x24 -> x0, waiting for transfers between devices: 41.9 us -> none  [the longest x12 39.5 us: with_halo(): after = lax.ppermute(initial, axis, down)]
    pallas_call x0 -> x1, Pallas kernels: none -> 39.9 us  [shards(): pl.pallas_call(kernel, out_shape=[jax.ShapeDtypeStruct((ROWS, COLS), F32)...]
    unnamed x6 -> x10, local copies, waits for them, and re-layouts: 0.01 us -> 5.02 us
  transfers between devices with their start and end apart: 24 -> 0, of which waited for: 14 -> 0; matrix products, arithmetic and copies ran while one was open for 0% -> 0% of each run, Pallas kernels for 0% -> 0%
where the time goes in v1:
time: 45.8 us; the launch traced here: 45.5 us
  Pallas kernels  39.9 us (87%)
  local copies, waits for them, and re-layouts  5.02 us (11%)
  between operations  0.65 us (1%)
    pallas_call x1, Pallas kernels, shards(): pl.pallas_call(kernel, out_shape=[jax.ShapeDtypeStruct((ROWS, COLS), F32)...  39.9 us
    unnamed x10, local copies, waits for them, and re-layouts  5.02 us

profile of v1, /device:TPU:1, one launch (start us, length us, event | category | flops | bytes accessed | tf_op | source)
XLA Modules:
  0.0 45.5 jit_solution(17915698925837708247)
XLA Ops:
  0.6 0.0 copy-start.3
  0.6 0.7 %copy-done.3 = f32[8,2]{0,1:T(2,128)S(1)} copy-done((f32[8,2]{0,1:T(2,128)S(1)}, f32[8,2]{0,1:T(2,128)}, u32[]{:S(2)}) %copy-start.3) | copy-done | bytes 88
  1.3 0.0 copy-start
  1.3 1.2 %copy-done = f32[8,128,256]{2,1,0:T(8,128)S(1)} copy-done((f32[8,128,256]{2,1,0:T(8,128)S(1)}, f32[8,128,256]{2,1,0:T(8,128)}, u32[]{:S(2)}) %copy-start) | copy-done | bytes 1048600
  2.5 0.0 copy-start.1
  2.5 0.9 %copy-done.1 = f32[128,256]{1,0:T(8,128)S(1)} copy-done((f32[128,256]{1,0:T(8,128)S(1)}, f32[128,256]{1,0:T(8,128)}, u32[]{:S(2)}) %copy-start.1) | copy-done | bytes 131096
  3.4 0.0 copy-start.2
  3.4 0.9 %copy-done.2 = f32[128,256]{1,0:T(8,128)S(1)} copy-done((f32[128,256]{1,0:T(8,128)S(1)}, f32[128,256]{1,0:T(8,128)}, u32[]{:S(2)}) %copy-start.2) | copy-done | bytes 131096
  4.3 39.9 %shard_map.59 = (f32[128,256]{1,0:T(8,128)S(1)}, f32[128,256]{1,0:T(8,128)S(1)}) custom-call(f32[128,256]{1,0:T(8,128)S(1)} %copy-done.1, f32[128,256]{1,0:T(8,128)S(1)} %copy-done.2, f32[8,128,256]{2,1,0:T(8,128)S(1)} %copy-done, f32[2,8]{1,0:T(2,128)S(1)} %bitcast.1), custom_call_target="tpu_custom_call" | custom-call | tf_op jit(solution)/shard_map/pallas_call | solution.py:328
  44.2 0.7 %copy.8 = f32[128,256]{1,0:T(8,128)} copy(f32[128,256]{1,0:T(8,128)S(1)} %get-tuple-element.4) | data formatting | bytes 262144
  44.9 0.7 %copy.9 = f32[128,256]{1,0:T(8,128)} copy(f32[128,256]{1,0:T(8,128)S(1)} %get-tuple-element.5) | data formatting | bytes 262144
Async XLA Ops:
  0.6 0.7 %copy-start.3 = (f32[8,2]{0,1:T(2,128)S(1)}, f32[8,2]{0,1:T(2,128)}, u32[]{:S(2)}) copy-start(f32[8,2]{0,1:T(2,128)} %param.7) | copy-start | bytes 196
  1.3 1.2 %copy-start = (f32[8,128,256]{2,1,0:T(8,128)S(1)}, f32[8,128,256]{2,1,0:T(8,128)}, u32[]{:S(2)}) copy-start(f32[8,128,256]{2,1,0:T(8,128)} %images.1) | copy-start | bytes 3145732
  2.5 0.9 %copy-start.1 = (f32[128,256]{1,0:T(8,128)S(1)}, f32[128,256]{1,0:T(8,128)}, u32[]{:S(2)}) copy-start(f32[128,256]{1,0:T(8,128)} %heights.1) | copy-start | bytes 393220
  3.4 0.9 %copy-start.2 = (f32[128,256]{1,0:T(8,128)S(1)}, f32[128,256]{1,0:T(8,128)}, u32[]{:S(2)}) copy-start(f32[128,256]{1,0:T(8,128)} %albedo.1) | copy-start | bytes 393220

commit v2 on v1

--- a/solution.py
+++ b/solution.py
@@ -259,12 +259,12 @@
             acc = (acc[0] + r * r, acc[1] + r * u, acc[2] + u * u, acc[3] + u * w)
         return acc
 
-    lax.fori_loop(0, TILES + 2, linearize, 0, unroll=2)
-    lax.fori_loop(0, TILES + 2, right_side, 0, unroll=3)
-    lax.fori_loop(0, TILES + 2, apply_from(vec_r), 0, unroll=2)
-    lax.fori_loop(0, TILES + 2, image_of_r, 0, unroll=3)
-    lax.fori_loop(0, TILES + 2, apply_from(vec_u), 0, unroll=2)
-    acc = lax.fori_loop(1, TILES + 1, image_of_u, (zero, zero, zero, zero), unroll=4)
+    lax.fori_loop(0, TILES + 2, linearize, 0, unroll=9)
+    lax.fori_loop(0, TILES + 2, right_side, 0, unroll=9)
+    lax.fori_loop(0, TILES + 2, apply_from(vec_r), 0, unroll=9)
+    lax.fori_loop(0, TILES + 2, image_of_r, 0, unroll=9)
+    lax.fori_loop(0, TILES + 2, apply_from(vec_u), 0, unroll=9)
+    acc = lax.fori_loop(1, TILES + 1, image_of_u, (zero, zero, zero, zero), unroll=16)
 
     folded = []
     for x in acc:
@@ -351,7 +351,7 @@
             pltpu.SemaphoreType.DMA((2,)),
             pltpu.SemaphoreType.DMA((2,)),
         ],
-        compiler_params=pltpu.CompilerParams(collective_id=0, has_side_effects=True, vmem_limit_bytes=40 * 1024 * 1024),
+        compiler_params=pltpu.CompilerParams(collective_id=0, has_side_effects=True, vmem_limit_bytes=56 * 1024 * 1024),
     )(heights, albedo, images, lights.T)
 
 

time: 45.8 us -> 39.2 us (0.86)
  Pallas kernels: 39.9 us -> 36.1 us
  local copies, waits for them, and re-layouts: 5.02 us -> 2.26 us
    pallas_call x1, Pallas kernels: 39.9 us -> 36.1 us  [shards(): pl.pallas_call(kernel, out_shape=[jax.ShapeDtypeStruct((ROWS, COLS), F32)...]
    unnamed x10 -> x4, local copies, waits for them, and re-layouts: 5.02 us -> 2.26 us
where the time goes in v2:
time: 39.2 us; the launch traced here: 39 us
  Pallas kernels  36.1 us (92%)
  local copies, waits for them, and re-layouts  2.26 us (6%)
  between operations  0.65 us (2%)
    pallas_call x1, Pallas kernels, shards(): pl.pallas_call(kernel, out_shape=[jax.ShapeDtypeStruct((ROWS, COLS), F32)...  36.1 us
    unnamed x4, local copies, waits for them, and re-layouts  2.26 us

profile of v2, /device:TPU:1, one launch (start us, length us, event | category | flops | bytes accessed | tf_op | source)
XLA Modules:
  0.0 39.0 jit_solution(2786728383654205019)
XLA Ops:
  0.6 36.1 %shard_map.59 = (f32[128,256]{1,0:T(8,128)}, f32[128,256]{1,0:T(8,128)}) custom-call(f32[128,256]{1,0:T(8,128)} %heights.1, f32[128,256]{1,0:T(8,128)} %albedo.1, f32[8,128,256]{2,1,0:T(8,128)} %images.1, f32[2,8]{1,0:T(2,128)} %bitcast.1), custom_call_target="tpu_custom_call" | custom-call | tf_op jit(solution)/shard_map/pallas_call | solution.py:328
  36.8 0.0 copy-start
  36.8 1.6 %copy.8 = f32[128,256]{1,0:T(8,128)} copy(f32[128,256]{1,0:T(8,128)} %get-tuple-element.4) | data formatting | bytes 262144
  38.4 0.0 copy-done
  38.4 0.7 %copy.9 = f32[128,256]{1,0:T(8,128)} copy(f32[128,256]{1,0:T(8,128)S(1)} %copy-done) | data formatting | bytes 262144
Async XLA Ops:
  36.8 1.6 %copy-start = (f32[128,256]{1,0:T(8,128)S(1)}, f32[128,256]{1,0:T(8,128)}, u32[]{:S(2)}) copy-start(f32[128,256]{1,0:T(8,128)} %get-tuple-element.5) | copy-start | bytes 393220

commit v3 on v1

v3 whole, which is shorter than its diff:
```python
import jax
import jax.numpy as jnp
from jax import lax
from jax.experimental import pallas as pl
from jax.experimental.pallas import tpu as pltpu
from jax.sharding import PartitionSpec as P

MESH = pl.DeviceIdType.MESH
F32 = jnp.float32
NIMG = 8
NR, NC = 16, 32
ROWS, COLS = 128, 256
TILES = ROWS // 8
NF = 5
TOP = 16
UN = (4, 8, 7, 4, 9)
STRIDE = 12


def kernel(
    heights, albedo, images, lights, sol_out, res_out,
    fields, img, light, packs, strips, corners, rows_in, coef, xs, yp, ym, vec_r, vec_u, krylov, part, sums_row, sums_col,
    in_sem, img_sem, send_sem, recv_sem, ar_send, ar_recv,
):
    row, col = lax.axis_index("row"), lax.axis_index("col")

    def dev(dr, dc):
        return (lax.rem(row + (dr + NR), NR), lax.rem(col + (dc + NC), NC))

    loads = []
    for f, src in enumerate((heights, albedo)):
        for t in range(2):
            loads.append(
                pltpu.make_async_copy(src.at[:, pl.ds(128 * t, 128)], fields.at[f, t, pl.ds(TOP, ROWS), :], in_sem.at[2 * f + t])
            )
    load_light = pltpu.make_async_copy(lights, light, in_sem.at[4])
    load_img = [pltpu.make_async_copy(images.at[k], img.at[k], img_sem.at[k]) for k in range(NIMG)]
    load_light.start()
    for cp in load_img:
        cp.start()
    for cp in loads:
        cp.start()

    peers = {(a, b) for a in (-1, 0, 1) for b in (-1, 0, 1)} | {(d, 0) for d in range(NR)} | {(0, d) for d in range(NC)}
    peers = sorted({(a % NR, b % NC) for a, b in peers} - {(0, 0)})
    barrier = pltpu.get_barrier_semaphore()
    for p in peers:
        pl.semaphore_signal(barrier, inc=1, device_id=dev(*p), device_id_type=MESH)

    lane = lax.broadcasted_iota(jnp.int32, (8, 128), 1)
    zero = jnp.zeros((8, 128), F32)

    load_light.wait()
    lx, ly = light[0:1, :], light[1:2, :]
    inv_sq = 1.0 / (1.0 + lx * lx + ly * ly)
    inv_norm = jnp.sqrt(inv_sq)

    def over_images(x):
        return jnp.broadcast_to(jnp.sum(x, axis=1, keepdims=True), (8, 128))

    m00, m10, m01 = over_images(inv_sq), over_images(inv_sq * lx), over_images(inv_sq * ly)
    m20, m11, m02 = over_images(inv_sq * lx * lx), over_images(inv_sq * lx * ly), over_images(inv_sq * ly * ly)
    weights = [
        [jnp.broadcast_to(w[:, k : k + 1], (8, 128)) for w in (inv_norm, inv_norm * lx, inv_norm * ly)] for k in range(NIMG)
    ]

    for cp in load_img:
        cp.wait()

    def image_sums(i, carry):
        at = pl.ds(pl.multiple_of(8 * i, 8), 8)
        to = pl.ds(pl.multiple_of(8 * i + TOP, 8), 8)
        for t in range(2):
            acc = [zero, zero, zero]
            for k in range(NIMG):
                v = img[k, at, pl.ds(128 * t, 128)]
                acc = [acc[j] + weights[k][j] * v for j in range(3)]
            for j in range(3):
                fields[2 + j, t, to, :] = acc[j]
        return carry

    lax.fori_loop(0, TILES, image_sums, 0, unroll=2)
    for cp in loads:
        cp.wait()

    def tile(e):
        return pl.ds(pl.multiple_of(8 * e + 8, 8), 8)

    shifts = [(64 * g + STRIDE * f, g, f) for g in range(2) for f in range(NF)]

    def pack(j, carry):
        left, right, first = zero, zero, None
        for s, g, f in shifts:
            a = fields[f, 0, tile(j + (8 * g + 1)), :]
            b = fields[f, 1, tile(j + (8 * (1 - g) + 1)), :]
            if s:
                a, b = pltpu.roll(a, s, 1), pltpu.roll(b, s, 1)
                left = jnp.where(lane >= s, a, left)
                right = jnp.where(lane >= s - 6, b, right)
            else:
                left, right, first = a, b, b
        to = pl.ds(pl.multiple_of(8 * j, 8), 8)
        packs[0, to, :] = left
        packs[1, to, :] = jnp.where(lane >= 122, first, right)
        return carry

    lax.fori_loop(0, 8, pack, 0, unroll=4)

    pl.semaphore_wait(barrier, len(peers))
    first8, last8 = pl.ds(0, 8), pl.ds(56, 8)
    moves = [
        (packs.at[0, first8, :], corners.at[1, 0], (-1, -1)),
        (packs.at[1, first8, :], corners.at[1, 1], (-1, 1)),
        (packs.at[0, last8, :], corners.at[0, 0], (1, -1)),
        (packs.at[1, last8, :], corners.at[0, 1], (1, 1)),
        (fields.at[:, pl.ds(0, 2), pl.ds(TOP, 8), :], rows_in.at[1], (-1, 0)),
        (fields.at[:, pl.ds(0, 2), pl.ds(TOP + ROWS - 8, 8), :], rows_in.at[0], (1, 0)),
        (packs.at[0], strips.at[0], (0, -1)),
        (packs.at[1], strips.at[1], (0, 1)),
    ]
    copies = [
        pltpu.make_async_remote_copy(
            src_ref=src, dst_ref=dst, send_sem=send_sem.at[n], recv_sem=recv_sem.at[n], device_id=dev(*to), device_id_type=MESH
        )
        for n, (src, dst, to) in enumerate(moves)
    ]
    for cp in copies:
        cp.start()

    above = jnp.where(row > 0, 1.0, 0.0).astype(F32)
    below = jnp.where(row < NR - 1, 1.0, 0.0).astype(F32)
    before = jnp.where(col > 0, 1.0, 0.0).astype(F32)
    after = jnp.where(col < NC - 1, 1.0, 0.0).astype(F32)
    side_mask = jnp.where(lane < 64, jnp.where(lane < 32, after, before), 1.0)
    is_last, is_first = lane == 127, lane == 0

    def row_mask(e):
        return jnp.where(e == 0, above, jnp.where(e == TILES + 1, below, 1.0))

    def nexts(v):
        r = [pltpu.roll(x, 127, 1) for x in v]
        return [jnp.where(is_last, r[1], r[0]), r[1]] if len(v) == 2 else r

    def prevs(v):
        r = [pltpu.roll(x, 1, 1) for x in v]
        return [r[0], jnp.where(is_first, r[0], r[1])] if len(v) == 2 else r

    def scatter(k, ts, e, q, hx, hy):
        n = nexts([a - b for a, b in zip(q, hx)])
        p = prevs([a + b for a, b in zip(q, hx)])
        for i, t in enumerate(ts):
            xs[k, t, tile(e), :] = n[i] + p[i] - 4.0 * q[i]
            yp[k, t, tile(e), :] = q[i] - hy[i]
            ym[k, t, tile(e), :] = q[i] + hy[i]

    def stencil(ref, ts, e, mask):
        v = [ref[t, tile(e), :] for t in ts]
        up = [ref[t, pl.ds(8 * e + 7, 8), :] for t in ts]
        down = [ref[t, pl.ds(8 * e + 9, 8), :] for t in ts]
        n, p = nexts(v), prevs(v)
        quarter = 0.25 if mask is None else 0.25 * mask
        q = [quarter * ((a + b) + (c + d) - 4.0 * x) for a, b, c, d, x in zip(n, p, up, down, v)]
        return v, q, [a - b for a, b in zip(n, p)], [a - b for a, b in zip(down, up)]

    def gather(k, t, e):
        return xs[k, t, tile(e), :] + yp[k, t, pl.ds(8 * e + 9, 8), :] + ym[k, t, pl.ds(8 * e + 7, 8), :]

    def mask_of(ts, e, inner):
        if inner:
            return None
        return row_mask(e) * side_mask if ts == (2,) else row_mask(e)

    def linearize(ts, inner, e):
        _, q, gx, gy = stencil(fields.at[0], ts, e, mask_of(ts, e, inner))
        hx, hy = [], []
        for i, t in enumerate(ts):
            sx, sy = 0.5 * gx[i], 0.5 * gy[i]
            inv = 1.0 / (1.0 + sx * sx + sy * sy)
            a = fields[1, t, tile(e), :] * jnp.sqrt(inv)
            j0, jx, jy = (fields[f, t, tile(e), :] for f in (2, 3, 4))
            tx, ty = sx * inv, sy * inv
            f1x = m10 - sx * m20 - sy * m11
            f1y = m01 - sx * m11 - sy * m02
            f2 = m00 - sx * m10 - sy * m01 - sx * f1x - sy * f1y
            g1x, g1y = f1x + tx * f2, f1y + ty * f2
            jf = j0 - sx * jx - sy * jy
            qa = 0.25 * (a * a)
            coef[0, t, tile(e), :] = qa * (m20 + tx * (f1x + g1x))
            coef[1, t, tile(e), :] = qa * (m11 + ty * f1x + tx * g1y)
            coef[2, t, tile(e), :] = qa * (m02 + ty * (f1y + g1y))
            ha = 0.5 * a
            hx.append(ha * (jx + tx * jf - a * g1x))
            hy.append(ha * (jy + ty * jf - a * g1y))
        scatter(0, ts, e, q, hx, hy)

    def right_side(ts, inner, e):
        m = mask_of(ts, e, inner)
        for t in ts:
            v = gather(0, t, e)
            vec_r[t, tile(e), :] = -v if m is None else -m * v

    def image_of_r(ts, inner, e):
        m = mask_of(ts, e, inner)
        for t in ts:
            v = gather(1, t, e)
            vec_u[t, tile(e), :] = v if m is None else m * v

    def weighted(ref, ts, e, mask):
        v, q, gx, gy = stencil(ref, ts, e, mask)
        cxx, cxy, cyy = ([coef[j, t, tile(e), :] for t in ts] for j in range(3))
        hx = [a * x + b * y for a, b, x, y in zip(cxx, cxy, gx, gy)]
        hy = [a * x + b * y for a, b, x, y in zip(cxy, cyy, gx, gy)]
        return v, q, gx, gy, hx, hy

    def apply_r(ts, inner, e):
        _, q, _, _, hx, hy = weighted(vec_r, ts, e, mask_of(ts, e, inner))
        scatter(1, ts, e, q, hx, hy)

    counts = {0: lane >= 8, 1: lane < 120, 2: ((lane >= 64) & (lane < 72)) | (lane >= 120)}

    def apply_u(ts, inner, e, acc, own=None):
        u, q, gx, gy, hx, hy = weighted(vec_u, ts, e, mask_of(ts, e, inner))
        scatter(2, ts, e, q, hx, hy)
        for i, t in enumerate(ts):
            ok = counts[t] if own is None else counts[t] & own
            r = vec_r[t, tile(e), :]
            terms = (r * r, r * u[i], u[i] * u[i], gx[i] * hx[i] + gy[i] * hy[i] + 4.0 * (q[i] * q[i]))
            acc = tuple(a + jnp.where(ok, x, 0.0) for a, x in zip(acc, terms))
        return acc

    def over(lo, hi, body, unroll):
        def step(e, carry):
            body(e)
            return carry

        lax.fori_loop(lo, hi, step, 0, unroll=unroll)

    main, edge = (0, 1), (2,)

    def own_edge(e):
        for f in range(NF):
            fields[f, 2, tile(e), :] = jnp.where(lane < 96, pltpu.roll(fields[f, 0, tile(e), :], 64, 1), fields[f, 1, tile(e), :])

    over(1, TILES + 1, own_edge, UN[0])
    over(1, TILES + 1, lambda e: linearize(main, True, e), UN[1])
    over(1, TILES + 1, lambda e: right_side(main, True, e), UN[1])
    over(1, TILES + 1, lambda e: apply_r(main, True, e), UN[1])
    over(1, TILES + 1, lambda e: image_of_r(main, True, e), UN[1])
    acc = lax.fori_loop(2, TILES, lambda e, acc: apply_u(main, True, e, acc), (zero, zero, zero, zero), unroll=UN[2])

    for cp in copies:
        cp.wait_recv()

    in_group = lane & 63
    from_right = in_group < 6
    for f in range(1, NF):
        from_right = from_right | ((in_group >= STRIDE * f) & (in_group < STRIDE * f + 6))

    def outer(merged, g, f):
        s = 64 * g + STRIDE * f
        return pltpu.roll(merged, 128 - s, 1) if s else merged

    def unpack(j):
        at = pl.ds(pl.multiple_of(8 * j, 8), 8)
        merged = jnp.where(from_right, strips[0, at, :], strips[1, at, :])
        for s, g, f in shifts:
            to = tile(j + (8 * g + 1))
            v = outer(merged, g, f)
            fields[f, 2, to, :] = jnp.where(lane < 64, v * side_mask if f < 2 else v, fields[f, 2, to, :])

    over(0, 8, unpack, UN[3])
    for b, g, e, ok in ((0, 1, 0, above), (1, 0, TILES + 1, below)):
        merged = jnp.where(from_right, corners[b, 0], corners[b, 1])
        for f in range(NF):
            v0, v1 = rows_in[b, f, 0], rows_in[b, f, 1]
            v = jnp.where(lane < 64, outer(merged, g, f), jnp.where(lane < 96, pltpu.roll(v0, 64, 1), v1))
            fields[f, 0, tile(e), :] = v0 * ok if f < 2 else v0
            fields[f, 1, tile(e), :] = v1 * ok if f < 2 else v1
            fields[f, 2, tile(e), :] = v * (side_mask * ok) if f < 2 else v

    def both(body):
        over(0, TILES + 2, lambda e: body(edge, False, e), UN[4])
        over(0, 4, lambda i: body(main, False, i + (TILES - 2) * (i // 2)), 4)

    both(linearize)
    both(right_side)
    both(apply_r)
    both(image_of_r)

    def inside(e):
        return (jnp.zeros((8, 128), jnp.int32) + e >= 1) & (jnp.zeros((8, 128), jnp.int32) + e <= TILES)

    acc = lax.fori_loop(0, TILES + 2, lambda e, acc: apply_u(edge, False, e, acc, inside(e)), acc, unroll=UN[4])

    def last_rows(i, acc):
        e = i + (TILES - 2) * (i // 2)
        return apply_u(main, False, e, acc, inside(e))

    acc = lax.fori_loop(0, 4, last_rows, acc, unroll=4)

    folded = []
    for x in acc:
        x = x + pltpu.roll(x, 64, 1)
        folded.append(x + pltpu.roll(x, 32, 1))
    mixed = jnp.where(lane < 64, jnp.where(lane < 32, folded[0], folded[1]), jnp.where(lane < 96, folded[2], folded[3]))
    mine = jnp.sum(mixed, axis=0, keepdims=True)

    def exchange(stage, mine, slots, count, target, meanwhile):
        part[stage] = mine
        out = [
            pltpu.make_async_remote_copy(
                src_ref=part.at[stage], dst_ref=slots.at[d - 1], send_sem=ar_send.at[stage], recv_sem=ar_recv.at[stage],
                device_id=target(d), device_id_type=MESH,
            )
            for d in range(1, count)
        ]
        for cp in out:
            cp.start()
        meanwhile()
        pltpu.make_async_copy(slots, slots, ar_recv.at[stage]).wait()
        total = mine
        for d in range(1, count):
            total = total + slots[d - 1]
        return total

    def joined(ref, e):
        side = ref[2, tile(e), :] if not isinstance(ref, int) else gather(ref, 2, e)
        inner = [ref[t, tile(e), :] if not isinstance(ref, int) else gather(ref, t, e) for t in main]
        return jnp.where(lane < 8, pltpu.roll(side, 64, 1), inner[0]), jnp.where(lane >= 120, side, inner[1])

    def merge(e):
        at = pl.ds(pl.multiple_of(8 * e - 8, 8), 8)
        for n, ref in enumerate((vec_r, vec_u, 2)):
            for t, v in enumerate(joined(ref, e)):
                krylov[n, at, pl.ds(128 * t, 128)] = v

    total = exchange(0, mine, sums_row, NR, lambda d: dev(d, 0), lambda: over(1, TILES + 1, merge, 4))

    def settle():
        for cp in copies:
            cp.wait_send()
        pltpu.make_async_copy(sums_row, sums_row, ar_send.at[0]).wait()

    total = exchange(1, total, sums_col, NC, lambda d: dev(0, d), settle)

    lane1 = lax.broadcasted_iota(jnp.int32, (1, 128), 1)

    def quarter(n):
        picked = jnp.where((lane1 >= 32 * n) & (lane1 < 32 * n + 32), total, 0.0)
        return jnp.broadcast_to(jnp.sum(picked, axis=1, keepdims=True), (8, 128))

    rr, ru, uu, uw = (quarter(n) for n in range(4))
    p1, p2, p3 = ru / rr, uu / rr, uw / rr
    step0 = 1.0 / (1.0 + p1)
    keep = p1 * step0
    beta = (p2 - p1 * p1) * (step0 * step0)
    g = keep + beta
    curve = g * g * (1.0 + p1) - 2.0 * g * step0 * (p1 + p2) + step0 * step0 * (p2 + p3)
    step1 = beta / curve
    s_r, s_u = step0 + step1 * g, -step1 * step0
    d_r, d_u, d_w = keep - step1 * g, -step0 - step1 * (g - step0), step1 * step0

    def finish(i):
        at = pl.ds(pl.multiple_of(8 * i, 8), 8)
        for t in range(2):
            lanes = pl.ds(128 * t, 128)
            r, u, w = (krylov[n, at, lanes] for n in range(3))
            sol_out[at, lanes] = s_r * r + s_u * u
            res_out[at, lanes] = d_r * r + d_u * u + d_w * w

    over(0, TILES, finish, 4)
    pltpu.make_async_copy(sums_col, sums_col, ar_send.at[1]).wait()


def shards(heights, albedo, images, lights):
    padded = pltpu.VMEM((3, ROWS + 32, 128), F32)
    stacked = pltpu.VMEM((3, 3, ROWS + 32, 128), F32)
    return pl.pallas_call(
        kernel,
        out_shape=[jax.ShapeDtypeStruct((ROWS, COLS), F32)] * 2,
        in_specs=[pl.BlockSpec(memory_space=pltpu.HBM)] * 4,
        out_specs=[pl.BlockSpec(memory_space=pltpu.VMEM)] * 2,
        scratch_shapes=[
            pltpu.VMEM((NF, 3, ROWS + 32, 128), F32),
            pltpu.VMEM((NIMG, ROWS, COLS), F32),
            pltpu.VMEM((2, NIMG), F32),
            pltpu.VMEM((2, ROWS // 2, 128), F32),
            pltpu.VMEM((2, ROWS // 2, 128), F32),
            pltpu.VMEM((2, 2, 8, 128), F32),
            pltpu.VMEM((2, NF, 2, 8, 128), F32),
            stacked,
            stacked, stacked, stacked,
            padded, padded,
            pltpu.VMEM((3, ROWS, COLS), F32),
            pltpu.VMEM((2, 1, 128), F32),
            pltpu.VMEM((NR - 1, 1, 128), F32),
            pltpu.VMEM((NC - 1, 1, 128), F32),
            pltpu.SemaphoreType.DMA((5,)),
            pltpu.SemaphoreType.DMA((NIMG,)),
            pltpu.SemaphoreType.DMA((8,)),
            pltpu.SemaphoreType.DMA((8,)),
            pltpu.SemaphoreType.DMA((2,)),
            pltpu.SemaphoreType.DMA((2,)),
        ],
        compiler_params=pltpu.CompilerParams(collective_id=0, has_side_effects=True, vmem_limit_bytes=40 * 1024 * 1024),
    )(*(pltpu.with_memory_space_constraint(x, pltpu.HBM) for x in (heights, albedo, images, lights.T)))


def solution(mesh):
    placed = (P("row", "col"), P("row", "col"), P(None, "row", "col"), P())
    return jax.shard_map(
        shards, mesh=mesh, in_specs=placed, out_specs=(P("row", "col"), P("row", "col")), check_vma=False
    )
```

time: 45.8 us -> 37.1 us (0.81)
  Pallas kernels: 39.9 us -> 35 us
  local copies, waits for them, and re-layouts: 5.02 us -> 1.31 us
    pallas_call x1, Pallas kernels: 39.9 us -> 35 us  [shards(): pl.pallas_call(kernel, out_shape=[jax.ShapeDtypeStruct((ROWS, COLS), F32)...]
    unnamed x10 -> x2, local copies, waits for them, and re-layouts: 5.02 us -> 1.31 us
where the time goes in v3:
time: 37.1 us; the launch traced here: 37 us
  Pallas kernels  35 us (94%)
  local copies, waits for them, and re-layouts  1.31 us (4%)
  between operations  0.64 us (2%)
    pallas_call x1, Pallas kernels, shards(): pl.pallas_call(kernel, out_shape=[jax.ShapeDtypeStruct((ROWS, COLS), F32)...  35 us
    unnamed x2, local copies, waits for them, and re-layouts  1.31 us

profile of v3, /device:TPU:1, one launch (start us, length us, event | category | flops | bytes accessed | tf_op | source)
XLA Modules:
  0.0 37.0 jit_solution(1155845449486262252)
XLA Ops:
  0.6 35.0 %shard_map.59 = (f32[128,256]{1,0:T(8,128)S(1)}, f32[128,256]{1,0:T(8,128)S(1)}) custom-call(f32[128,256]{1,0:T(8,128)} %heights.1, f32[128,256]{1,0:T(8,128)} %albedo.1, f32[8,128,256]{2,1,0:T(8,128)} %images.1, f32[2,8]{1,0:T(2,128)} %bitcast.1), custom_call_target="tpu_custom_call" | custom-call | tf_op jit(solution)/shard_map/pallas_call | solution.py:378
  35.6 0.7 %copy.8 = f32[128,256]{1,0:T(8,128)} copy(f32[128,256]{1,0:T(8,128)S(1)} %get-tuple-element.4) | data formatting | bytes 262144
  36.3 0.7 %copy.9 = f32[128,256]{1,0:T(8,128)} copy(f32[128,256]{1,0:T(8,128)S(1)} %get-tuple-element.5) | data formatting | bytes 262144

commit v4 on v3

--- a/solution.py
+++ b/solution.py
@@ -11,14 +11,19 @@
 NR, NC = 16, 32
 ROWS, COLS = 128, 256
 TILES = ROWS // 8
+HALF = TILES // 2 + 1
 NF = 5
 TOP = 16
 UN = (4, 8, 7, 4, 9)
 STRIDE = 12
 
 
+def around(d, count):
+    return min(d % count, -d % count)
+
+
 def kernel(
-    heights, albedo, images, lights, sol_out, res_out,
+    heights, albedo, images, lights, out,
     fields, img, light, packs, strips, corners, rows_in, coef, xs, yp, ym, vec_r, vec_u, krylov, part, sums_row, sums_col,
     in_sem, img_sem, send_sem, recv_sem, ar_send, ar_recv,
 ):
@@ -26,6 +31,13 @@
 
     def dev(dr, dc):
         return (lax.rem(row + (dr + NR), NR), lax.rem(col + (dc + NC), NC))
+
+    peers = {(a, b) for a in (-1, 0, 1) for b in (-1, 0, 1)} | {(d, 0) for d in range(NR)} | {(0, d) for d in range(NC)}
+    peers = {(a % NR, b % NC) for a, b in peers} - {(0, 0)}
+    peers = sorted(peers, key=lambda p: (p[0] == 0, -around(p[0], NR), -around(p[1], NC), p))
+    barrier = pltpu.get_barrier_semaphore()
+    for p in peers:
+        pl.semaphore_signal(barrier, inc=1, device_id=dev(*p), device_id_type=MESH)
 
     loads = []
     for f, src in enumerate((heights, albedo)):
@@ -40,12 +52,6 @@
         cp.start()
     for cp in loads:
         cp.start()
-
-    peers = {(a, b) for a in (-1, 0, 1) for b in (-1, 0, 1)} | {(d, 0) for d in range(NR)} | {(0, d) for d in range(NC)}
-    peers = sorted({(a % NR, b % NC) for a, b in peers} - {(0, 0)})
-    barrier = pltpu.get_barrier_semaphore()
-    for p in peers:
-        pl.semaphore_signal(barrier, inc=1, device_id=dev(*p), device_id_type=MESH)
 
     lane = lax.broadcasted_iota(jnp.int32, (8, 128), 1)
     zero = jnp.zeros((8, 128), F32)
@@ -279,8 +285,14 @@
             fields[f, 2, tile(e), :] = v * (side_mask * ok) if f < 2 else v
 
     def both(body):
-        over(0, TILES + 2, lambda e: body(edge, False, e), UN[4])
-        over(0, 4, lambda i: body(main, False, i + (TILES - 2) * (i // 2)), 4)
+        def step(i, carry):
+            for j in range(2):
+                body(main, False, TILES * i + j)
+            for j in range(HALF):
+                body(edge, False, HALF * i + j)
+            return carry
+
+        lax.fori_loop(0, 2, step, 0, unroll=2)
 
     both(linearize)
     both(right_side)
@@ -290,13 +302,14 @@
     def inside(e):
         return (jnp.zeros((8, 128), jnp.int32) + e >= 1) & (jnp.zeros((8, 128), jnp.int32) + e <= TILES)
 
-    acc = lax.fori_loop(0, TILES + 2, lambda e, acc: apply_u(edge, False, e, acc, inside(e)), acc, unroll=UN[4])
-
-    def last_rows(i, acc):
-        e = i + (TILES - 2) * (i // 2)
-        return apply_u(main, False, e, acc, inside(e))
-
-    acc = lax.fori_loop(0, 4, last_rows, acc, unroll=4)
+    def last(i, acc):
+        for j in range(2):
+            acc = apply_u(main, False, TILES * i + j, acc, inside(TILES * i + j))
+        for j in range(HALF):
+            acc = apply_u(edge, False, HALF * i + j, acc, inside(HALF * i + j))
+        return acc
+
+    acc = lax.fori_loop(0, 2, last, acc, unroll=2)
 
     folded = []
     for x in acc:
@@ -305,14 +318,14 @@
     mixed = jnp.where(lane < 64, jnp.where(lane < 32, folded[0], folded[1]), jnp.where(lane < 96, folded[2], folded[3]))
     mine = jnp.sum(mixed, axis=0, keepdims=True)
 
-    def exchange(stage, mine, slots, count, target, meanwhile):
+    def exchange(stage, mine, slots, count, target, far, meanwhile):
         part[stage] = mine
         out = [
             pltpu.make_async_remote_copy(
                 src_ref=part.at[stage], dst_ref=slots.at[d - 1], send_sem=ar_send.at[stage], recv_sem=ar_recv.at[stage],
                 device_id=target(d), device_id_type=MESH,
             )
-            for d in range(1, count)
+            for d in sorted(range(1, count), key=lambda d: -far(d))
         ]
         for cp in out:
             cp.start()
@@ -334,14 +347,14 @@
             for t, v in enumerate(joined(ref, e)):
                 krylov[n, at, pl.ds(128 * t, 128)] = v
 
-    total = exchange(0, mine, sums_row, NR, lambda d: dev(d, 0), lambda: over(1, TILES + 1, merge, 4))
+    total = exchange(0, mine, sums_row, NR, lambda d: dev(d, 0), lambda d: around(d // 4, 4) + around(d, 4), lambda: over(1, TILES + 1, merge, 4))
 
     def settle():
         for cp in copies:
             cp.wait_send()
         pltpu.make_async_copy(sums_row, sums_row, ar_send.at[0]).wait()
 
-    total = exchange(1, total, sums_col, NC, lambda d: dev(0, d), settle)
+    total = exchange(1, total, sums_col, NC, lambda d: dev(0, d), lambda d: around(d, NC), settle)
 
     lane1 = lax.broadcasted_iota(jnp.int32, (1, 128), 1)
 
@@ -365,8 +378,8 @@
         for t in range(2):
             lanes = pl.ds(128 * t, 128)
             r, u, w = (krylov[n, at, lanes] for n in range(3))
-            sol_out[at, lanes] = s_r * r + s_u * u
-            res_out[at, lanes] = d_r * r + d_u * u + d_w * w
+            out[0, at, lanes] = s_r * r + s_u * u
+            out[1, at, lanes] = d_r * r + d_u * u + d_w * w
 
     over(0, TILES, finish, 4)
     pltpu.make_async_copy(sums_col, sums_col, ar_send.at[1]).wait()
@@ -375,11 +388,11 @@
 def shards(heights, albedo, images, lights):
     padded = pltpu.VMEM((3, ROWS + 32, 128), F32)
     stacked = pltpu.VMEM((3, 3, ROWS + 32, 128), F32)
-    return pl.pallas_call(
+    out = pl.pallas_call(
         kernel,
-        out_shape=[jax.ShapeDtypeStruct((ROWS, COLS), F32)] * 2,
+        out_shape=jax.ShapeDtypeStruct((2, ROWS, COLS), F32),
         in_specs=[pl.BlockSpec(memory_space=pltpu.HBM)] * 4,
-        out_specs=[pl.BlockSpec(memory_space=pltpu.VMEM)] * 2,
+        out_specs=pl.BlockSpec(memory_space=pltpu.VMEM),
         scratch_shapes=[
             pltpu.VMEM((NF, 3, ROWS + 32, 128), F32),
             pltpu.VMEM((NIMG, ROWS, COLS), F32),
@@ -404,6 +417,7 @@
         ],
         compiler_params=pltpu.CompilerParams(collective_id=0, has_side_effects=True, vmem_limit_bytes=40 * 1024 * 1024),
     )(*(pltpu.with_memory_space_constraint(x, pltpu.HBM) for x in (heights, albedo, images, lights.T)))
+    return out[0], out[1]
 
 
 def solution(mesh):

time: 37.1 us -> 35.6 us (0.960)
  Pallas kernels: 35 us -> 34.1 us
  local copies, waits for them, and re-layouts: 1.31 us -> 0.72 us
    unnamed x2 -> x0, local copies, waits for them, and re-layouts: 1.31 us -> none
    pallas_call x1, Pallas kernels: 35 us -> 34.1 us  [shards(): pl.pallas_call(kernel, out_shape=jax.ShapeDtypeStruct((2, ROWS, COLS), F3...]
    squeeze x0 -> x1, local copies, waits for them, and re-layouts: none -> 0.72 us  [shards(): return (out[0], out[1])]
where the time goes in v4:
time: 35.6 us; the launch traced here: 35.4 us
  Pallas kernels  34.1 us (96%)
  local copies, waits for them, and re-layouts  0.72 us (2%)
  between operations  0.64 us (2%)
    pallas_call x1, Pallas kernels, shards(): pl.pallas_call(kernel, out_shape=jax.ShapeDtypeStruct((2, ROWS, COLS), F3...  34.1 us
    squeeze x1, local copies, waits for them, and re-layouts, shards(): return (out[0], out[1])  0.72 us

profile of v4, /device:TPU:1, one launch (start us, length us, event | category | flops | bytes accessed | tf_op | source)
XLA Modules:
  0.0 35.4 jit_solution(10675810333650441581)
XLA Ops:
  0.6 34.1 %shard_map.59 = f32[2,128,256]{2,1,0:T(8,128)S(1)} custom-call(f32[128,256]{1,0:T(8,128)} %heights.1, f32[128,256]{1,0:T(8,128)} %albedo.1, f32[8,128,256]{2,1,0:T(8,128)} %images.1, f32[2,8]{1,0:T(2,128)} %bitcast.5), custom_call_target="tpu_custom_call" | custom-call | tf_op jit(solution)/shard_map/pallas_call | solution.py:391
  34.7 0.7 %slice_bitcast_fusion = (f32[128,256]{1,0:T(8,128)}, f32[128,256]{1,0:T(8,128)}) fusion(f32[2,128,256]{2,1,0:T(8,128)S(1)} %shard_map.59), kind=kLoop, calls=%fused_computation | loop fusion | bytes 524288 | tf_op jit(solution)/shard_map/squeeze | solution.py:420

commit v5 on v4

--- a/solution.py
+++ b/solution.py
@@ -14,7 +14,7 @@
 HALF = TILES // 2 + 1
 NF = 5
 TOP = 16
-UN = (4, 8, 7, 4, 9)
+UN = (4, 8, 7, 8, 9)
 STRIDE = 12
 
 
@@ -24,7 +24,7 @@
 
 def kernel(
     heights, albedo, images, lights, out,
-    fields, img, light, packs, strips, corners, rows_in, coef, xs, yp, ym, vec_r, vec_u, krylov, part, sums_row, sums_col,
+    fields, img, light, packs, strips, corners, rows_in, coef, xs, yp, ym, vec_r, vec_u, krylov, part, sums_row, sums_col, sums_all,
     in_sem, img_sem, send_sem, recv_sem, ar_send, ar_recv,
 ):
     row, col = lax.axis_index("row"), lax.axis_index("col")
@@ -38,6 +38,17 @@
     barrier = pltpu.get_barrier_semaphore()
     for p in peers:
         pl.semaphore_signal(barrier, inc=1, device_id=dev(*p), device_id_type=MESH)
+
+    first = (row == 0) & (col == 1)
+
+    @pl.when(first)
+    def _():
+        def greet(i, carry):
+            n = lax.rem(i + 2, NR * NC)
+            pl.semaphore_signal(barrier, inc=1, device_id=(n // NC, lax.rem(n, NC)), device_id_type=MESH)
+            return carry
+
+        lax.fori_loop(0, NR * NC - 1, greet, 0, unroll=7)
 
     loads = []
     for f, src in enumerate((heights, albedo)):
@@ -112,7 +123,14 @@
 
     lax.fori_loop(0, 8, pack, 0, unroll=4)
 
-    pl.semaphore_wait(barrier, len(peers))
+    @pl.when(first)
+    def _():
+        pl.semaphore_wait(barrier, len(peers))
+
+    @pl.when(jnp.logical_not(first))
+    def _():
+        pl.semaphore_wait(barrier, len(peers) + 1)
+
     first8, last8 = pl.ds(0, 8), pl.ds(56, 8)
     moves = [
         (packs.at[0, first8, :], corners.at[1, 0], (-1, -1)),
@@ -318,23 +336,17 @@
     mixed = jnp.where(lane < 64, jnp.where(lane < 32, folded[0], folded[1]), jnp.where(lane < 96, folded[2], folded[3]))
     mine = jnp.sum(mixed, axis=0, keepdims=True)
 
-    def exchange(stage, mine, slots, count, target, far, meanwhile):
-        part[stage] = mine
-        out = [
+    def sends(stage, slots, count, target, far):
+        return [
             pltpu.make_async_remote_copy(
                 src_ref=part.at[stage], dst_ref=slots.at[d - 1], send_sem=ar_send.at[stage], recv_sem=ar_recv.at[stage],
                 device_id=target(d), device_id_type=MESH,
             )
             for d in sorted(range(1, count), key=lambda d: -far(d))
         ]
-        for cp in out:
-            cp.start()
-        meanwhile()
-        pltpu.make_async_copy(slots, slots, ar_recv.at[stage]).wait()
-        total = mine
-        for d in range(1, count):
-            total = total + slots[d - 1]
-        return total
+
+    def await_bytes(slots, sem):
+        pltpu.make_async_copy(slots, slots, sem).wait()
 
     def joined(ref, e):
         side = ref[2, tile(e), :] if not isinstance(ref, int) else gather(ref, 2, e)
@@ -347,15 +359,65 @@
             for t, v in enumerate(joined(ref, e)):
                 krylov[n, at, pl.ds(128 * t, 128)] = v
 
-    total = exchange(0, mine, sums_row, NR, lambda d: dev(d, 0), lambda d: around(d // 4, 4) + around(d, 4), lambda: over(1, TILES + 1, merge, 4))
-
-    def settle():
-        for cp in copies:
-            cp.wait_send()
-        pltpu.make_async_copy(sums_row, sums_row, ar_send.at[0]).wait()
-
-    total = exchange(1, total, sums_col, NC, lambda d: dev(0, d), lambda d: around(d, NC), settle)
-
+    part[0] = mine
+    direct = pltpu.make_async_remote_copy(
+        src_ref=part.at[0], dst_ref=sums_all.at[row * NC + col], send_sem=ar_send.at[2], recv_sem=ar_recv.at[2],
+        device_id=(0, 1), device_id_type=MESH,
+    )
+
+    @pl.when(jnp.logical_not(first))
+    def _():
+        direct.start()
+
+    for cp in sends(0, sums_row, NR, lambda d: dev(d, 0), lambda d: around(d // 4, 4) + around(d, 4)):
+        cp.start()
+    over(1, TILES + 1, merge, 4)
+    await_bytes(sums_row, ar_recv.at[0])
+    total = mine
+    for d in range(1, NR):
+        total = total + sums_row[d - 1]
+    part[1] = total
+
+    @pl.when((row > 0) | first)
+    def _():
+        for cp in sends(1, sums_col, NC, lambda d: dev(0, d), lambda d: around(d, NC)):
+            cp.start()
+
+    @pl.when((row == 0) & (col != 1))
+    def _():
+        for d in sorted(range(1, NC), key=lambda d: -around(d, NC)):
+            @pl.when(lax.rem(col + d, NC) != 1)
+            def _():
+                pltpu.make_async_remote_copy(
+                    src_ref=part.at[1], dst_ref=sums_col.at[d - 1], send_sem=ar_send.at[1], recv_sem=ar_recv.at[1],
+                    device_id=dev(0, d), device_id_type=MESH,
+                ).start()
+
+    for cp in copies:
+        cp.wait_send()
+    await_bytes(sums_row, ar_send.at[0])
+
+    @pl.when(jnp.logical_not(first))
+    def _():
+        direct.wait_send()
+        await_bytes(sums_col, ar_recv.at[1])
+        total = part[1]
+        for d in range(1, NC):
+            total = total + sums_col[d - 1]
+        part[2] = total
+
+    @pl.when(first)
+    def _():
+        await_bytes(sums_all.at[pl.ds(0, NR * NC - 1)], ar_recv.at[2])
+        sums_all[1] = part[0]
+
+        def add(i, acc):
+            return tuple(x + sums_all[8 * i + j] for j, x in enumerate(acc))
+
+        acc = lax.fori_loop(0, NR * NC // 8, add, (jnp.zeros((1, 128), F32),) * 8, unroll=8)
+        part[2] = ((acc[0] + acc[1]) + (acc[2] + acc[3])) + ((acc[4] + acc[5]) + (acc[6] + acc[7]))
+
+    total = part[2]
     lane1 = lax.broadcasted_iota(jnp.int32, (1, 128), 1)
 
     def quarter(n):
@@ -382,7 +444,14 @@
             out[1, at, lanes] = d_r * r + d_u * u + d_w * w
 
     over(0, TILES, finish, 4)
-    pltpu.make_async_copy(sums_col, sums_col, ar_send.at[1]).wait()
+
+    @pl.when((row > 0) | first)
+    def _():
+        await_bytes(sums_col, ar_send.at[1])
+
+    @pl.when((row == 0) & (col != 1))
+    def _():
+        await_bytes(sums_col.at[pl.ds(0, NC - 2)], ar_send.at[1])
 
 
 def shards(heights, albedo, images, lights):
@@ -405,15 +474,16 @@
             stacked, stacked, stacked,
             padded, padded,
             pltpu.VMEM((3, ROWS, COLS), F32),
-            pltpu.VMEM((2, 1, 128), F32),
+            pltpu.VMEM((3, 1, 128), F32),
             pltpu.VMEM((NR - 1, 1, 128), F32),
             pltpu.VMEM((NC - 1, 1, 128), F32),
+            pltpu.VMEM((NR * NC, 1, 128), F32),
             pltpu.SemaphoreType.DMA((5,)),
             pltpu.SemaphoreType.DMA((NIMG,)),
             pltpu.SemaphoreType.DMA((8,)),
             pltpu.SemaphoreType.DMA((8,)),
-            pltpu.SemaphoreType.DMA((2,)),
-            pltpu.SemaphoreType.DMA((2,)),
+            pltpu.SemaphoreType.DMA((3,)),
+            pltpu.SemaphoreType.DMA((3,)),
         ],
         compiler_params=pltpu.CompilerParams(collective_id=0, has_side_effects=True, vmem_limit_bytes=40 * 1024 * 1024),
     )(*(pltpu.with_memory_space_constraint(x, pltpu.HBM) for x in (heights, albedo, images, lights.T)))

time: 35.6 us -> 33.7 us (0.947)
  Pallas kernels: 34.1 us -> 31.9 us
    pallas_call x1, Pallas kernels: 34.1 us -> 31.9 us  [shards(): pl.pallas_call(kernel, out_shape=jax.ShapeDtypeStruct((2, ROWS, COLS), F3...]
where the time goes in v5:
time: 33.7 us; the launch traced here: 33.2 us
  Pallas kernels  31.9 us (95%)
  local copies, waits for them, and re-layouts  0.72 us (2%)
  between operations  0.64 us (2%)
    pallas_call x1, Pallas kernels, shards(): pl.pallas_call(kernel, out_shape=jax.ShapeDtypeStruct((2, ROWS, COLS), F3...  31.9 us
    squeeze x1, local copies, waits for them, and re-layouts, shards(): return (out[0], out[1])  0.72 us

profile of v5, /device:TPU:1, one launch (start us, length us, event | category | flops | bytes accessed | tf_op | source)
XLA Modules:
  0.0 33.2 jit_solution(8683540508378852936)
XLA Ops:
  0.6 31.9 %shard_map.59 = f32[2,128,256]{2,1,0:T(8,128)S(1)} custom-call(f32[128,256]{1,0:T(8,128)} %heights.1, f32[128,256]{1,0:T(8,128)} %albedo.1, f32[8,128,256]{2,1,0:T(8,128)} %images.1, f32[2,8]{1,0:T(2,128)} %bitcast.5), custom_call_target="tpu_custom_call" | custom-call | tf_op jit(solution)/shard_map/pallas_call | solution.py:460
  32.5 0.7 %slice_bitcast_fusion = (f32[128,256]{1,0:T(8,128)}, f32[128,256]{1,0:T(8,128)}) fusion(f32[2,128,256]{2,1,0:T(8,128)S(1)} %shard_map.59), kind=kLoop, calls=%fused_computation | loop fusion | bytes 524288 | tf_op jit(solution)/shard_map/squeeze | solution.py:490

commit v6 on v5

--- a/solution.py
+++ b/solution.py
@@ -96,7 +96,7 @@
                 fields[2 + j, t, to, :] = acc[j]
         return carry
 
-    lax.fori_loop(0, TILES, image_sums, 0, unroll=2)
+    lax.fori_loop(0, TILES, image_sums, 0, unroll=4)
     for cp in loads:
         cp.wait()
 
@@ -121,7 +121,7 @@
         packs[1, to, :] = jnp.where(lane >= 122, first, right)
         return carry
 
-    lax.fori_loop(0, 8, pack, 0, unroll=4)
+    lax.fori_loop(0, 8, pack, 0, unroll=8)
 
     @pl.when(first)
     def _():
@@ -194,8 +194,8 @@
             return None
         return row_mask(e) * side_mask if ts == (2,) else row_mask(e)
 
-    def linearize(ts, inner, e):
-        _, q, gx, gy = stencil(fields.at[0], ts, e, mask_of(ts, e, inner))
+    def linearize(ts, inner, e, mask=None):
+        _, q, gx, gy = stencil(fields.at[0], ts, e, mask if inner else mask_of(ts, e, inner))
         hx, hy = [], []
         for i, t in enumerate(ts):
             sx, sy = 0.5 * gx[i], 0.5 * gy[i]
@@ -272,7 +272,7 @@
     over(1, TILES + 1, lambda e: image_of_r(main, True, e), UN[1])
     acc = lax.fori_loop(2, TILES, lambda e, acc: apply_u(main, True, e, acc), (zero, zero, zero, zero), unroll=UN[2])
 
-    for cp in copies:
+    for cp in copies[6:]:
         cp.wait_recv()
 
     in_group = lane & 63
@@ -293,6 +293,9 @@
             fields[f, 2, to, :] = jnp.where(lane < 64, v * side_mask if f < 2 else v, fields[f, 2, to, :])
 
     over(0, 8, unpack, UN[3])
+    over(2, TILES, lambda e: linearize(edge, True, e, side_mask), TILES - 2)
+    for cp in copies[:6]:
+        cp.wait_recv()
     for b, g, e, ok in ((0, 1, 0, above), (1, 0, TILES + 1, below)):
         merged = jnp.where(from_right, corners[b, 0], corners[b, 1])
         for f in range(NF):
@@ -312,7 +315,13 @@
 
         lax.fori_loop(0, 2, step, 0, unroll=2)
 
-    both(linearize)
+    def linearize_rows(i, carry):
+        for j in range(2):
+            linearize(main, False, TILES * i + j)
+            linearize(edge, False, TILES * i + j)
+        return carry
+
+    lax.fori_loop(0, 2, linearize_rows, 0, unroll=2)
     both(right_side)
     both(apply_r)
     both(image_of_r)
@@ -443,7 +452,7 @@
             out[0, at, lanes] = s_r * r + s_u * u
             out[1, at, lanes] = d_r * r + d_u * u + d_w * w
 
-    over(0, TILES, finish, 4)
+    over(0, TILES, finish, 16)
 
     @pl.when((row > 0) | first)
     def _():

time: 33.7 us -> 33.5 us (level)
  no operation moved by 1% of the time
where the time goes in v6:
time: 33.5 us; the launch traced here: 33 us
  Pallas kernels  31.7 us (95%)
  local copies, waits for them, and re-layouts  0.72 us (2%)
  between operations  0.64 us (2%)
    pallas_call x1, Pallas kernels, shards(): pl.pallas_call(kernel, out_shape=jax.ShapeDtypeStruct((2, ROWS, COLS), F3...  31.7 us
    squeeze x1, local copies, waits for them, and re-layouts, shards(): return (out[0], out[1])  0.72 us

profile of v6, /device:TPU:1, one launch (start us, length us, event | category | flops | bytes accessed | tf_op | source)
XLA Modules:
  0.0 33.0 jit_solution(11077964784427956680)
XLA Ops:
  0.6 31.7 %shard_map.59 = f32[2,128,256]{2,1,0:T(8,128)S(1)} custom-call(f32[128,256]{1,0:T(8,128)} %heights.1, f32[128,256]{1,0:T(8,128)} %albedo.1, f32[8,128,256]{2,1,0:T(8,128)} %images.1, f32[2,8]{1,0:T(2,128)} %bitcast.5), custom_call_target="tpu_custom_call" | custom-call | tf_op jit(solution)/shard_map/pallas_call | solution.py:469
  32.3 0.7 %slice_bitcast_fusion = (f32[128,256]{1,0:T(8,128)}, f32[128,256]{1,0:T(8,128)}) fusion(f32[2,128,256]{2,1,0:T(8,128)S(1)} %shard_map.59), kind=kLoop, calls=%fused_computation | loop fusion | bytes 524288 | tf_op jit(solution)/shard_map/squeeze | solution.py:499

commit v7 on v6

--- a/solution.py
+++ b/solution.py
@@ -148,8 +148,8 @@
         )
         for n, (src, dst, to) in enumerate(moves)
     ]
-    for cp in copies:
-        cp.start()
+    for n in (4, 5, 0, 1, 2, 3, 6, 7):
+        copies[n].start()
 
     above = jnp.where(row > 0, 1.0, 0.0).astype(F32)
     below = jnp.where(row < NR - 1, 1.0, 0.0).astype(F32)

time: 33.5 us -> 33.5 us (level)
  no operation moved by 1% of the time
where the time goes in v7:
time: 33.5 us; the launch traced here: 33 us
  Pallas kernels  31.7 us (95%)
  local copies, waits for them, and re-layouts  0.72 us (2%)
  between operations  0.64 us (2%)
    pallas_call x1, Pallas kernels, shards(): pl.pallas_call(kernel, out_shape=jax.ShapeDtypeStruct((2, ROWS, COLS), F3...  31.7 us
    squeeze x1, local copies, waits for them, and re-layouts, shards(): return (out[0], out[1])  0.72 us

profile of v7, /device:TPU:1, one launch (start us, length us, event | category | flops | bytes accessed | tf_op | source)
XLA Modules:
  0.0 33.0 jit_solution(5616601681812398712)
XLA Ops:
  0.6 31.7 %shard_map.59 = f32[2,128,256]{2,1,0:T(8,128)S(1)} custom-call(f32[128,256]{1,0:T(8,128)} %heights.1, f32[128,256]{1,0:T(8,128)} %albedo.1, f32[8,128,256]{2,1,0:T(8,128)} %images.1, f32[2,8]{1,0:T(2,128)} %bitcast.5), custom_call_target="tpu_custom_call" | custom-call | tf_op jit(solution)/shard_map/pallas_call | solution.py:469
  32.3 0.7 %slice_bitcast_fusion = (f32[128,256]{1,0:T(8,128)}, f32[128,256]{1,0:T(8,128)}) fusion(f32[2,128,256]{2,1,0:T(8,128)S(1)} %shard_map.59), kind=kLoop, calls=%fused_computation | loop fusion | bytes 524288 | tf_op jit(solution)/shard_map/squeeze | solution.py:499
